TPU v7x, 128 devices: a whole 4x4x4 slice. The times are simulated.
128 devices in a mesh: img: 8 (over z, y_hi), ref: 16 (over x, y_lo, core).
Axes of the slice: x: 4, y: 4 (y_hi: 2, y_lo: 2; y = y_hi * 2 + y_lo), z: 4, core: 2. Of those that a mesh axis runs over, the one named last changes fastest.
Arguments:
- images: bfloat16 [8192, 9216], P(('img', 'ref')), may hold values from -96 to 96
- references: bfloat16 [6912, 9216], P('ref'), may hold values from -0.5 to 0.5
- class_prior: float32 [192], P('ref'), may hold values from 0.2 to 5
Outputs:
- class_sums: float32 [192, 9216], P('ref', 'img')
- class_weights: float32 [192], P('ref')
All inputs are finite; a program needn't handle non-finite values.
Results may differ from a plain program's by a relative error of at most 0.0021.
Values may be sent and summed in bfloat16 or wider, within the bound.
A program may use at most 128 MiB of HBM per device.

v0:
```python
import math
import numpy as np
import jax
import jax.numpy as jnp
from jax import lax
from jax.sharding import PartitionSpec as P

ANG = 144
ROT = 36
TURN = 4


def real_dft():
    b = np.arange(ROT)
    rows = []
    for f in range(1, ROT // 2):
        rows.append(np.cos(2 * np.pi * f * b / ROT))
        rows.append(-np.sin(2 * np.pi * f * b / ROT))
    rows = [np.ones(ROT), (-1.0) ** b] + rows
    return np.array(rows).astype(np.float32)


def real_idft():
    b = np.arange(ROT)
    rows = [np.ones(ROT) / ROT, (-1.0) ** b / ROT]
    for f in range(1, ROT // 2):
        rows.append(2 * np.cos(2 * np.pi * f * b / ROT) / ROT)
        rows.append(-2 * np.sin(2 * np.pi * f * b / ROT) / ROT)
    return np.array(rows).T.astype(np.float32)


def per_device(images, references, class_prior):
    hi = lax.Precision.HIGHEST
    classes_here = class_prior.shape[0]
    n_img, pixels = images.shape
    rad = pixels // ANG
    templates = references.reshape(classes_here, ROT, pixels)[:, 0]
    half_norm = 0.5 * jnp.sum(jnp.square(templates.astype(jnp.float32)), axis=1)
    offset = jnp.log(class_prior) - half_norm
    offsets = lax.all_gather(offset, "ref", axis=0, tiled=True)
    tall = lax.all_gather(templates, "ref", axis=0, tiled=True)
    k = tall.shape[0]
    dft, idft = (real_dft(), real_idft())
    x5 = images.reshape(n_img, rad, ROT, TURN).transpose(2, 0, 1, 3).reshape(ROT, n_img, rad * TURN)
    t5 = tall.reshape(k, rad, ROT, TURN).transpose(2, 0, 1, 3).reshape(ROT, k, rad * TURN)
    xh = jnp.einsum("jb,bnc->jnc", dft, x5.astype(jnp.float32), precision=hi)
    th = jnp.einsum("jb,bkc->jkc", dft, t5.astype(jnp.float32), precision=hi)
    xr, xi = (xh[0::2], xh[1::2])
    tr, ti = (th[0::2], th[1::2])
    dot = lambda a, b: jnp.einsum("fkc,fnc->fkn", a, b, precision=hi)
    rr, ii = (dot(tr, xr), dot(ti, xi))
    ri, ir = (dot(tr[1:], xi[1:]), dot(ti[1:], xr[1:]))
    sr = jnp.concatenate([rr[:1], rr[1:] + ii[1:]])
    si = jnp.concatenate([ii[:1], ri - ir])
    sh = jnp.stack([sr, si], axis=1).reshape(ROT, k, n_img)
    scores = jnp.einsum("rj,jkn->rkn", idft, sh, precision=hi) + offsets[None, :, None]
    top = jnp.max(scores, axis=(0, 1))
    e = jnp.exp(scores - top)
    weights = (e / jnp.sum(e, axis=(0, 1))).astype(jnp.bfloat16).astype(jnp.float32)
    mass = jnp.sum(weights, axis=(0, 2))
    class_weights = lax.psum_scatter(lax.psum(mass, "img"), "ref", scatter_dimension=0, tiled=True)
    wh = jnp.einsum("jr,rkn->jkn", dft, weights, precision=hi)
    wr, wi = (wh[0::2], wh[1::2])
    dot2 = lambda a, b: jnp.einsum("fkn,fnc->fkc", a, b, precision=hi)
    cr = jnp.concatenate([dot2(wr[:1], xr[:1]), dot2(wr[1:], xr[1:]) + dot2(wi[1:], xi[1:])])
    ci = jnp.concatenate([dot2(wi[:1], xi[:1]), dot2(wr[1:], xi[1:]) - dot2(wi[1:], xr[1:])])
    c = jnp.stack([cr, ci], axis=1).reshape(ROT, k, rad, TURN)
    sums = jnp.einsum("bj,jkqc->kqbc", idft, c, precision=hi).reshape(k, pixels)
    sums = lax.psum_scatter(sums, "ref", scatter_dimension=0, tiled=True)
    class_sums = lax.psum_scatter(sums, "img", scatter_dimension=1, tiled=True)
    return (class_sums, class_weights)


def solution(mesh):
    placed = (P(("img", "ref"), None), P("ref", None), P("ref"))
    return jax.shard_map(
        per_device,
        mesh=mesh,
        in_specs=placed,
        out_specs=(P("ref", "img"), P("ref")),
        check_vma=False,
    )
```

profile of v0, /device:TPU:0, one launch (start us, length us, event | category | flops | bytes accessed | tf_op | source)
XLA Modules:
  0.0 636.5 jit_solution(5112398509001411555)
XLA Ops:
  7.2 8.7 %reshape.45 = bf16[12,36,9216]{2,1,0:T(8,128)(2,1)} reshape(bf16[432,9216]{1,0:T(8,128)(2,1)} %param.9) | data formatting | bytes 15925248 | tf_op jit(solution)/shard_map/reshape | solution.py:37
  15.9 2.5 slice.90
  18.5 2.4 copy.58
  20.9 2.9 copy.59
  23.8 3.4 copy.60
  27.3 2.5 fusion.40
  29.8 4.8 slice.75
  34.6 4.9 slice.71
  39.5 1.7 slice.96
  41.2 1.1 slice.104
  43.8 2.1 multiply_reduce_fusion
  46.0 30.8 %all-reduce = f32[192]{0:T(256)S(1)} all-reduce(f32[192]{0:T(256)S(1)} %subtract_dynamic-update-slice_fusion), channel_id=1, replica_groups=mesh['img'=8,'ref'=16] {'ref'}, use_global_device_ids=true, to_apply=%add | all-reduce | flops 192 | bytes 1536
  76.8 16.0 %copy.55 = bf16[192,1,9216]{0,2,1:T(8,128)(2,1)} copy(bf16[192,1,9216]{2,1,0:T(2,128)(2,1)} %all-gather.3.cloned.1.call-done) | data formatting | bytes 7077888 | tf_op jit(solution)/shard_map/all_gather | solution.py:41
  92.8 7.9 %reshape.46 = bf16[192,64,36,4]{0,3,2,1:T(4,128)(2,1)} reshape(bf16[192,1,9216]{0,2,1:T(8,128)(2,1)} %copy.55) | data formatting | bytes 7077888 | tf_op jit(solution)/shard_map/reshape | solution.py:45
  100.7 7.0 %copy.56 = bf16[36,192,64,4]{1,3,2,0:T(4,128)(2,1)} copy(bf16[36,192,64,4]{1,3,0,2:T(4,128)(2,1)} %bitcast.63) | data formatting | bytes 7077888 | tf_op jit(solution)/shard_map/transpose | solution.py:45
  107.7 8.5 %reshape.47 = bf16[36,192,256]{1,2,0:T(8,128)(2,1)} reshape(bf16[36,192,64,4]{1,3,2,0:T(4,128)(2,1)} %copy.56) | data formatting | bytes 7077888 | tf_op jit(solution)/shard_map/reshape | solution.py:45
  116.2 7.9 %copy.57 = bf16[36,192,256]{2,0,1:T(8,128)(2,1)} copy(bf16[36,192,256]{1,2,0:T(8,128)(2,1)} %reshape.47) | data formatting | bytes 7077888 | tf_op jit(solution)/shard_map/reshape | solution.py:45
  124.1 8.4 %fusion.39 = f32[36,192,256]{2,0,1:T(8,128)} fusion(f32[36,36,1]{1,0,2:T(8,128)S(1)} %copy-done.6, bf16[36,192,256]{2,0,1:T(8,128)(2,1)} %copy.57), kind=kOutput, calls=%fused_computation.56 | convolution fusion | flops 764411904 | bytes 10622016 | tf_op jit(solution)/shard_map/jb,bkc->jkc/dot_general | solution.py:47
  132.5 22.0 %slice.74 = f32[18,192,256]{2,0,1:T(8,128)} slice(f32[36,192,256]{2,0,1:T(8,128)} %fusion.39), slice={[1:36:2], [0:192:1], [0:256:1]} | slice | bytes 7077888 | tf_op jit(solution)/shard_map/slice | solution.py:49
  154.5 22.2 %slice.70 = f32[18,192,256]{2,0,1:T(8,128)} slice(f32[36,192,256]{2,0,1:T(8,128)} %fusion.39), slice={[0:36:2], [0:192:1], [0:256:1]} | slice | bytes 7077888 | tf_op jit(solution)/shard_map/slice | solution.py:49
  176.7 7.8 %fusion = f32[18,192,64]{1,2,0:T(8,128)S(1)} fusion(f32[18,192,256]{2,0,1:T(8,128)} %slice.74, f32[18,64,256]{2,0,1:T(8,128)} %slice.75), kind=kOutput, calls=%fused_computation.4 | convolution fusion | flops 679477248 | bytes 5603328 | tf_op jit(solution)/shard_map/fkc,fnc->fkn/dot_general | solution.py:50
  184.5 3.4 slice.97
  187.9 4.9 fusion.2
  194.0 5.1 fusion.4
  199.1 4.6 fusion.11
  204.9 4.3 add_reduce_fusion
  210.2 1.5 convert_reduce_fusion
  211.7 2.7 fusion.14
  214.4 8.1 %slice.82 = f32[18,192,64]{1,0,2:T(8,128)} slice(f32[36,192,64]{1,0,2:T(8,128)} %fusion.14), slice={[0:36:2], [0:192:1], [0:64:1]} | slice | bytes 1769472 | tf_op jit(solution)/shard_map/slice | solution.py:63
  222.5 8.1 %slice.86 = f32[18,192,64]{1,0,2:T(8,128)} slice(f32[36,192,64]{1,0,2:T(8,128)} %fusion.14), slice={[1:36:2], [0:192:1], [0:64:1]} | slice | bytes 1769472 | tf_op jit(solution)/shard_map/slice | solution.py:63
  230.6 1.7 slice.102
  232.3 1.1 slice.103
  233.5 3.4 fusion.20
  236.9 3.4 fusion.22
  240.3 3.4 convolution_subtract_fusion
  243.8 3.7 convolution_add_fusion
  248.9 3.4 pad_maximum_fusion
  252.2 14.4 %copy.84 = f32[18,2,192,256]{2,1,0,3:T(2,128)} copy(f32[18,2,192,256]{3,2,0,1:T(8,128)} %pad_maximum_fusion) | data formatting | bytes 14155776 | tf_op jit(solution)/shard_map/reshape | solution.py:67
  266.6 12.4 %reshape.69 = f32[36,192,64,4]{1,0,3,2:T(8,128)} reshape(f32[18,2,192,256]{2,1,0,3:T(2,128)} %copy.84) | data formatting | bytes 14155776 | tf_op jit(solution)/shard_map/reshape | solution.py:67
  279.0 14.2 %convolution_bitcast_fusion = f32[192,64,36,4]{0,2,3,1:T(8,128)} fusion(f32[36,192,64,4]{1,0,3,2:T(8,128)} %reshape.69, f32[36,36,1,1]{1,0,3,2:T(8,128)S(1)} %copy-done.7), kind=kOutput, calls=%fused_computation.1 | convolution fusion | flops 764411904 | bytes 14160960 | tf_op jit(solution)/shard_map/bj,jkqc->kqbc/dot_general | solution.py:68
  293.2 11.9 %copy.81 = f32[192,64,36,4]{0,3,2,1:T(4,128)} copy(f32[192,64,36,4]{0,2,3,1:T(8,128)} %convolution_bitcast_fusion) | data formatting | bytes 14155776 | tf_op jit(solution)/shard_map/bj,jkqc->kqbc/transpose | solution.py:68
  305.1 12.0 %reshape.56 = f32[192,9216]{0,1:T(8,128)} reshape(f32[192,64,36,4]{0,3,2,1:T(4,128)} %copy.81) | data formatting | bytes 14155776 | tf_op jit(solution)/shard_map/reshape | solution.py:68
  317.8 212.6 %all-reduce.5.cloned.1.call-done = f32[192,9216]{0,1:T(8,128)} async-done(((f32[192,9216]{0,1:T(8,128)}), f32[192,9216]{0,1:T(8,128)}) %all-reduce.5.cloned.1.call-update) | async-done | bytes 7077904
  530.5 6.0 constant_dynamic-slice_fusion
  536.4 29.7 %all-reduce.2 = f32[192]{0:T(256)S(1)} all-reduce(f32[192]{0:T(256)S(1)} %get-tuple-element.6), channel_id=5, replica_groups=mesh['img'=8,'ref'=16] {'ref'}, use_global_device_ids=true, to_apply=%region_7.0.clone | all-reduce | flops 192 | bytes 1536
  566.2 25.2 %psum.8 = f32[12]{0:T(128)} all-reduce(f32[12]{0:T(128)S(1)} %dynamic-slice.4), channel_id=1, replica_groups=mesh['img'=8,'ref'=16] {'img'}, use_global_device_ids=true, to_apply=%region_6.0 | all-reduce | flops 12 | bytes 96 | tf_op jit(solution)/shard_map/psum | solution.py:61
  591.4 36.2 %reduce-scatter.3.cloned.1.call-done = f32[12,1152]{0,1:T(8,128)} async-done(((f32[12,9216]{0,1:T(8,128)}), f32[12,1152]{0,1:T(8,128)}) %reduce-scatter.3.cloned.1.call-update) | async-done | bytes 55312 | tf_op jit(solution)/shard_map/reduce_scatter | solution.py:70
  627.6 1.9 copy.82
  (56 shorter events, 6.1 us)
Async XLA Ops:
  7.2 11.3 %copy-start.5 = (bf16[64,9216]{1,0:T(8,128)(2,1)S(1)}, bf16[64,9216]{1,0:T(8,128)(2,1)}, u32[]{:S(2)}) copy-start(bf16[64,9216]{1,0:T(8,128)(2,1)} %param.8) | copy-start | bytes 3538948
  7.2 69.6 %all-gather.3.cloned.1.call-start = ((), (), s32[]{:S(2)}) async-start(), calls=%async_computation.2 | async-start | bytes 7520256 | tf_op jit(solution)/shard_map/all_gather | solution.py:41
  18.4 512.0 %all-reduce.5.cloned.1.call-start = ((), (), s32[]{:S(2)}) async-start(), calls=%async_computation.3 | async-start | bytes 18874368
  23.8 3.4 copy-start.6
  39.5 2.9 copy-start
  41.2 1.3 copy-start.9
  41.2 4.7 copy-start.10
  176.7 11.2 %slice-start = ((s8[4718592]{0:T(1024)(128)(4,1)}), s8[4194304]{0:T(1024)(128)(4,1)S(1)}, s32[]{:S(2)}) async-start(s8[4718592]{0:T(1024)(128)(4,1)} %bitcast.61), calls=%async_computation.4 | async-start | bytes 8388608
  184.5 9.5 %copy-start.3 = (f32[18,192,64]{1,2,0:T(8,128)}, f32[18,192,64]{1,2,0:T(8,128)S(1)}, u32[]{:S(2)}) copy-start(f32[18,192,64]{1,2,0:T(8,128)S(1)} %fusion) | copy-start | bytes 2654212
  184.5 3.4 slice-start.1
  184.5 3.4 copy-start.1
  192.8 1.0 copy-start.4
  199.1 4.6 slice-start.2
  199.1 4.6 slice-start.3
  204.2 0.7 copy-start.8
  230.6 2.8 copy-start.2
  266.6 12.4 %copy-start.7 = (f32[36,36,1,1]{1,0,3,2:T(8,128)S(1)}, f32[36,36,1,1]{1,0,3,2:T(8,128)}, u32[]{:S(2)}) copy-start(f32[36,36,1,1]{1,0,3,2:T(8,128)} %constant.30) | copy-start | bytes 15556
  317.1 310.5 %reduce-scatter.3.cloned.1.call-start = ((), (), s32[]{:S(2)}) async-start(), calls=%async_computation.1 | async-start | bytes 5308416 | tf_op jit(solution)/shard_map/reduce_scatter | solution.py:70
Sparse Core Ops, SparseCore 0:
  18.5 48.8 all-gather.2
  317.2 213.1 all-reduce.4
  536.6 91.0 reduce-scatter.2
where the time goes:
time: 649 us; the launch traced here: 637 us
  waiting for transfers between devices  249 us (38%)
  local copies, waits for them, and re-layouts  208 us (32%)
  blocking collectives  85.7 us (13%)
  matrix products  69 us (11%)
  between operations  15.9 us (2%)
  other arithmetic  9.31 us (1%)
    unnamed x4, waiting for transfers between devices  213 us
    unnamed x2, blocking collectives  60.5 us
    slice x2, local copies, waits for them, and re-layouts, per_device(): tr, ti = (th[0::2], th[1::2])  44.2 us
    reduce_scatter x1, waiting for transfers between devices, per_device(): class_sums = lax.psum_scatter(sums, 'img', scatter_dimension=1, tiled=True)  36.2 us
    reshape x2, local copies, waits for them, and re-layouts, per_device(): c = jnp.stack([cr, ci], axis=1).reshape(ROT, k, rad, TURN)  26.8 us
    psum x1, blocking collectives, per_device(): lax.psum(mass, 'img')  25.2 us
    reshape x3, local copies, waits for them, and re-layouts, per_device(): tall.reshape(k, rad, ROT, TURN).transpose(2, 0, 1, 3)  24.3 us
    dot_general x4, matrix products, per_device(): dot = lambda a, b: jnp.einsum('fkc,fnc->fkn', a, b, precision=hi)  22.4 us
  transfers between devices with their start and end apart: 3, of which 2 were waited for; matrix products, arithmetic and copies ran while one was open for 4% of the time, Pallas kernels for 0%

commit v1 on v0

--- a/solution.py
+++ b/solution.py
@@ -38,7 +38,9 @@
     half_norm = 0.5 * jnp.sum(jnp.square(templates.astype(jnp.float32)), axis=1)
     offset = jnp.log(class_prior) - half_norm
     offsets = lax.all_gather(offset, "ref", axis=0, tiled=True)
-    tall = lax.all_gather(templates, "ref", axis=0, tiled=True)
+    tall = jnp.concatenate(
+        lax.all_to_all(jnp.stack([templates] * lax.axis_size("ref")), "ref", 0, 0), axis=0
+    )
     k = tall.shape[0]
     dft, idft = (real_dft(), real_idft())
     x5 = images.reshape(n_img, rad, ROT, TURN).transpose(2, 0, 1, 3).reshape(ROT, n_img, rad * TURN)

time: 649 us -> 741 us (1.14)
  local copies, waits for them, and re-layouts: 208 us -> 266 us
  blocking collectives: 85.7 us -> 115 us
    another operation x0 -> x2, local copies, waits for them, and re-layouts: none -> 51.1 us  [the longest x1 48.4 us: per_device(): tall.reshape(k, rad, ROT, TURN).transpose(2, 0, 1, 3)]
    all_to_all x0 -> x1, local copies, waits for them, and re-layouts: none -> 32.2 us  [per_device(): lax.all_to_all(jnp.stack([templates] * lax.axis_size('ref')), 'ref', 0, 0)]
    unnamed x2, blocking collectives: 60.5 us -> 89.8 us
    all_gather x1 -> x0, local copies, waits for them, and re-layouts: 16 us -> none  [per_device(): tall = lax.all_gather(templates, 'ref', axis=0, tiled=True)]
    reshape x3 -> x2, local copies, waits for them, and re-layouts: 24.3 us -> 16.4 us  [per_device(): tall.reshape(k, rad, ROT, TURN).transpose(2, 0, 1, 3)]
    unnamed x4 -> x3, waiting for transfers between devices: 213 us -> 216 us
  transfers between devices with their start and end apart: 3 -> 3, of which waited for: 2 -> 2; matrix products, arithmetic and copies ran while one was open for 4% -> 3% of each run, Pallas kernels for 0% -> 0%
where the time goes in v1:
time: 741 us; the launch traced here: 731 us
  local copies, waits for them, and re-layouts  266 us (36%)
  waiting for transfers between devices  252 us (34%)
  blocking collectives  115 us (16%)
  matrix products  68.8 us (9%)
  between operations  15.9 us (2%)
  other arithmetic  7.51 us (1%)
    unnamed x3, waiting for transfers between devices  216 us
    unnamed x2, blocking collectives  89.8 us
    another operation x1, local copies, waits for them, and re-layouts, per_device(): tall.reshape(k, rad, ROT, TURN).transpose(2, 0, 1, 3)  48.4 us
    slice x2, local copies, waits for them, and re-layouts, per_device(): tr, ti = (th[0::2], th[1::2])  44.5 us
    reduce_scatter x1, waiting for transfers between devices, per_device(): class_sums = lax.psum_scatter(sums, 'img', scatter_dimension=1, tiled=True)  36.2 us
    all_to_all x1, local copies, waits for them, and re-layouts, per_device(): lax.all_to_all(jnp.stack([templates] * lax.axis_size('ref')), 'ref', 0, 0)  32.2 us
    reshape x2, local copies, waits for them, and re-layouts, per_device(): c = jnp.stack([cr, ci], axis=1).reshape(ROT, k, rad, TURN)  26.8 us
    psum x1, blocking collectives, per_device(): lax.psum(mass, 'img')  25.2 us
  transfers between devices with their start and end apart: 3, of which 2 were waited for; matrix products, arithmetic and copies ran while one was open for 3% of the time, Pallas kernels for 0%

profile of v1, /device:TPU:0, one launch (start us, length us, event | category | flops | bytes accessed | tf_op | source)
XLA Modules:
  0.0 731.4 jit_solution(374339643918801270)
XLA Ops:
  7.2 8.6 %reshape.44 = bf16[12,36,9216]{2,1,0:T(8,128)(2,1)} reshape(bf16[432,9216]{1,0:T(8,128)(2,1)} %param.9) | data formatting | bytes 15925248 | tf_op jit(solution)/shard_map/reshape | solution.py:37
  15.8 1.7 slice.90
  17.7 2.7 stack.21
  20.4 5.7 all-to-all-start
  26.1 2.4 copy.86
  28.5 2.9 copy.87
  31.5 3.4 copy.88
  34.9 2.5 fusion.40
  37.4 4.9 slice.75
  42.3 4.9 slice.71
  47.1 1.7 slice.96
  48.8 1.1 slice.104
  51.5 60.1 %all-reduce = f32[192]{0:T(256)S(1)} all-reduce(f32[192]{0:T(256)S(1)} %subtract_dynamic-update-slice_fusion), channel_id=1, replica_groups=mesh['img'=8,'ref'=16] {'ref'}, use_global_device_ids=true, to_apply=%add | all-reduce | flops 192 | bytes 1536
  111.6 32.2 %copy.83 = bf16[16,12,9216]{1,0,2:T(8,128)(2,1)} copy(bf16[16,12,9216]{2,1,0:T(8,128)(2,1)} %all-to-all-done) | data formatting | bytes 7077888 | tf_op jit(solution)/shard_map/all_to_all | solution.py:42
  143.8 48.4 %reshape_reshape.3 = bf16[192,64,36,4]{0,3,2,1:T(4,128)(2,1)} reshape(bf16[16,12,9216]{1,0,2:T(8,128)(2,1)} %copy.83) | data formatting | bytes 7077888 | tf_op jit(solution)/shard_map/reshape;reshape | solution.py:47
  192.2 7.0 copy.84
  199.2 8.5 %reshape.45 = bf16[36,192,256]{1,2,0:T(8,128)(2,1)} reshape(bf16[36,192,64,4]{1,3,2,0:T(4,128)(2,1)} %copy.84) | data formatting | bytes 7077888 | tf_op jit(solution)/shard_map/reshape | solution.py:47
  207.7 7.9 %copy.85 = bf16[36,192,256]{2,0,1:T(8,128)(2,1)} copy(bf16[36,192,256]{1,2,0:T(8,128)(2,1)} %reshape.45) | data formatting | bytes 7077888 | tf_op jit(solution)/shard_map/reshape | solution.py:47
  215.6 8.4 %fusion.39 = f32[36,192,256]{2,0,1:T(8,128)} fusion(f32[36,36,1]{1,0,2:T(8,128)S(1)} %copy-done.6, bf16[36,192,256]{2,0,1:T(8,128)(2,1)} %copy.85), kind=kOutput, calls=%fused_computation.57 | convolution fusion | flops 764411904 | bytes 10622016 | tf_op jit(solution)/shard_map/jb,bkc->jkc/dot_general | solution.py:49
  224.0 22.0 %slice.74 = f32[18,192,256]{2,0,1:T(8,128)} slice(f32[36,192,256]{2,0,1:T(8,128)} %fusion.39), slice={[1:36:2], [0:192:1], [0:256:1]} | slice | bytes 7077888 | tf_op jit(solution)/shard_map/slice | solution.py:51
  246.0 22.5 %slice.70 = f32[18,192,256]{2,0,1:T(8,128)} slice(f32[36,192,256]{2,0,1:T(8,128)} %fusion.39), slice={[0:36:2], [0:192:1], [0:256:1]} | slice | bytes 7077888 | tf_op jit(solution)/shard_map/slice | solution.py:51
  268.5 7.8 %fusion = f32[18,192,64]{1,2,0:T(8,128)S(1)} fusion(f32[18,192,256]{2,0,1:T(8,128)} %slice.74, f32[18,64,256]{2,0,1:T(8,128)} %slice.75), kind=kOutput, calls=%fused_computation.4 | convolution fusion | flops 679477248 | bytes 5603328 | tf_op jit(solution)/shard_map/fkc,fnc->fkn/dot_general | solution.py:52
  276.3 3.4 slice.97
  279.7 4.9 fusion.2
  285.9 4.8 fusion.4
  290.6 4.6 fusion.11
  296.4 4.3 add_reduce_fusion
  301.7 1.6 convert_reduce_fusion
  303.3 2.7 fusion.14
  306.0 8.1 %slice.82 = f32[18,192,64]{1,0,2:T(8,128)} slice(f32[36,192,64]{1,0,2:T(8,128)} %fusion.14), slice={[0:36:2], [0:192:1], [0:64:1]} | slice | bytes 1769472 | tf_op jit(solution)/shard_map/slice | solution.py:65
  314.1 8.1 %slice.86 = f32[18,192,64]{1,0,2:T(8,128)} slice(f32[36,192,64]{1,0,2:T(8,128)} %fusion.14), slice={[1:36:2], [0:192:1], [0:64:1]} | slice | bytes 1769472 | tf_op jit(solution)/shard_map/slice | solution.py:65
  322.2 1.7 slice.102
  325.1 3.4 fusion.20
  328.5 3.4 fusion.22
  331.9 3.4 convolution_subtract_fusion
  335.3 3.9 convolution_add_fusion
  340.6 3.4 pad_maximum_fusion
  344.0 14.4 %copy.112 = f32[18,2,192,256]{2,1,0,3:T(2,128)} copy(f32[18,2,192,256]{3,2,0,1:T(8,128)} %pad_maximum_fusion) | data formatting | bytes 14155776 | tf_op jit(solution)/shard_map/reshape | solution.py:69
  358.4 12.4 %reshape.63 = f32[36,192,64,4]{1,0,3,2:T(8,128)} reshape(f32[18,2,192,256]{2,1,0,3:T(2,128)} %copy.112) | data formatting | bytes 14155776 | tf_op jit(solution)/shard_map/reshape | solution.py:69
  370.8 14.1 %convolution_bitcast_fusion = f32[192,64,36,4]{0,2,3,1:T(8,128)} fusion(f32[36,192,64,4]{1,0,3,2:T(8,128)} %reshape.63, f32[36,36,1,1]{1,0,3,2:T(8,128)S(1)} %copy-done.7), kind=kOutput, calls=%fused_computation.1 | convolution fusion | flops 764411904 | bytes 14160960 | tf_op jit(solution)/shard_map/bj,jkqc->kqbc/dot_general | solution.py:70
  384.9 11.9 %copy.109 = f32[192,64,36,4]{0,3,2,1:T(4,128)} copy(f32[192,64,36,4]{0,2,3,1:T(8,128)} %convolution_bitcast_fusion) | data formatting | bytes 14155776 | tf_op jit(solution)/shard_map/bj,jkqc->kqbc/transpose | solution.py:70
  396.8 12.0 %reshape.54 = f32[192,9216]{0,1:T(8,128)} reshape(f32[192,64,36,4]{0,3,2,1:T(4,128)} %copy.109) | data formatting | bytes 14155776 | tf_op jit(solution)/shard_map/reshape | solution.py:70
  409.5 215.8 %all-reduce.5.cloned.1.call-done = f32[192,9216]{0,1:T(8,128)} async-done(((f32[192,9216]{0,1:T(8,128)}), f32[192,9216]{0,1:T(8,128)}) %all-reduce.5.cloned.1.call-update) | async-done | bytes 7077904
  625.3 6.0 constant_dynamic-slice_fusion
  631.2 29.7 %all-reduce.2 = f32[192]{0:T(256)S(1)} all-reduce(f32[192]{0:T(256)S(1)} %get-tuple-element.8), channel_id=4, replica_groups=mesh['img'=8,'ref'=16] {'ref'}, use_global_device_ids=true, to_apply=%region_7.0.clone | all-reduce | flops 192 | bytes 1536
  661.0 25.2 %psum.8 = f32[12]{0:T(128)} all-reduce(f32[12]{0:T(128)S(1)} %dynamic-slice.4), channel_id=1, replica_groups=mesh['img'=8,'ref'=16] {'img'}, use_global_device_ids=true, to_apply=%region_6.0 | all-reduce | flops 12 | bytes 96 | tf_op jit(solution)/shard_map/psum | solution.py:63
  686.2 36.2 %reduce-scatter.3.cloned.1.call-done = f32[12,1152]{0,1:T(8,128)} async-done(((f32[12,9216]{0,1:T(8,128)}), f32[12,1152]{0,1:T(8,128)}) %reduce-scatter.3.cloned.1.call-update) | async-done | bytes 55312 | tf_op jit(solution)/shard_map/reduce_scatter | solution.py:72
  722.4 1.9 copy.110
  (56 shorter events, 7.3 us)
Async XLA Ops:
  20.4 5.8 copy-start.5
  20.4 91.2 %all-to-all-start = ((bf16[16,12,9216]{2,1,0:T(8,128)(2,1)}), bf16[16,12,9216]{2,1,0:T(8,128)(2,1)}, u32[]{:S(2)}, u32[]{:S(2)}) async-start(bf16[16,12,9216]{2,1,0:T(8,128)(2,1)} %stack.21), calls=%async_computation | async-start | bytes 9437184 | tf_op jit(solution)/shard_map/all_to_all | solution.py:42
  26.1 599.2 %all-reduce.5.cloned.1.call-start = ((), (), s32[]{:S(2)}) async-start(), calls=%async_computation.3 | async-start | bytes 18874368
  31.5 3.4 copy-start.6
  47.1 2.8 copy-start
  48.8 1.3 copy-start.9
  48.8 2.6 copy-start.10
  268.5 11.2 %slice-start = ((s8[4718592]{0:T(1024)(128)(4,1)}), s8[4194304]{0:T(1024)(128)(4,1)S(1)}, s32[]{:S(2)}) async-start(s8[4718592]{0:T(1024)(128)(4,1)} %bitcast.64), calls=%async_computation.4 | async-start | bytes 8388608
  276.3 9.5 %copy-start.3 = (f32[18,192,64]{1,2,0:T(8,128)}, f32[18,192,64]{1,2,0:T(8,128)S(1)}, u32[]{:S(2)}) copy-start(f32[18,192,64]{1,2,0:T(8,128)S(1)} %fusion) | copy-start | bytes 2654212
  276.3 3.4 slice-start.1
  276.3 3.4 copy-start.1
  284.6 1.0 copy-start.4
  290.6 4.6 slice-start.2
  290.6 4.6 slice-start.3
  295.7 0.7 copy-start.8
  322.2 2.8 copy-start.2
  358.4 12.4 %copy-start.7 = (f32[36,36,1,1]{1,0,3,2:T(8,128)S(1)}, f32[36,36,1,1]{1,0,3,2:T(8,128)}, u32[]{:S(2)}) copy-start(f32[36,36,1,1]{1,0,3,2:T(8,128)} %constant.30) | copy-start | bytes 15556
  408.8 313.6 %reduce-scatter.3.cloned.1.call-start = ((), (), s32[]{:S(2)}) async-start(), calls=%async_computation.2 | async-start | bytes 5308416 | tf_op jit(solution)/shard_map/reduce_scatter | solution.py:72
Sparse Core Ops, SparseCore 0:
  408.9 216.2 all-reduce.4
  631.4 91.0 reduce-scatter.2
